TPU v7x, 1024 devices: a whole 8x8x8 slice. The times are simulated.
1024 devices in a mesh: rep: 64 (over x, y), exp: 16 (over z, core).
Axes of the slice: x: 8, y: 8, z: 8, core: 2. Of those that a mesh axis runs over, the one named last changes fastest.
Arguments:
- x_rows: bfloat16 [64, 2048, 2048], P('rep', 'exp'), may hold values from -8 to 8
- row_cot: bfloat16 [64, 2048, 2048], P('rep', 'exp'), may hold values from -8 to 8
- gate_vals: float32 [64, 2048], P('rep', 'exp'), may hold values from 0 to 1, as said below
- route_pos: int32 [64, 320, 4], P('rep', 'exp'), may hold values from 0 to 127, as said below
- weights: bfloat16 [16, 3, 2048, 384], P('exp'), may hold values from -0.125 to 0.125
- momentum: float32 [16, 3, 2048, 384], P('exp', None, 'rep'), may hold values from -6 to 6
Outputs:
- token_grad: bfloat16 [64, 320, 2048], P('rep', 'exp')
- momentum_new: float32 [16, 3, 2048, 384], P('exp', None, 'rep')
Inputs may be any that keep to these rules, and one draw needn't show every extreme that they name: `route_pos`: for each token of an owner, 4 positions e * 8 + c in ascending order, from 4 different experts e; from expert e an owner refers to slots c = 0 .. n - 1, each by exactly one token, where n is at most 8 and equals 8 for some expert of every owner; in every replica some owner uses all 8 slots of the last expert and some owner all of expert 0. `gate_vals`: row o * 8 + c of an expert in a replica belongs to owner o's slot c; its weight is zero exactly where no token of that owner refers to the slot, and positive elsewhere.
All inputs are finite; a program needn't handle non-finite values.
Results may differ from a plain program's by a relative error of at most 0.0064.
Values may be sent and summed in bfloat16 or wider, within the bound.
A program may use at most 64 MiB of HBM per device.

v0:
```python
import jax
import jax.numpy as jnp
from jax import lax
from jax.sharding import PartitionSpec as P

tiny_eps = 1e-06
moment_decay = 0.9


def from_partner(block, axis, distance):
    count = lax.axis_size(axis)
    route = []
    for low in range(count):
        high = low | 1 << distance
        if high != low and high < count:
            route += [(low, high), (high, low)]
    return lax.ppermute(block, axis, route)


def copy_for_each(value, axis):
    length = lax.axis_size(axis)
    return lax.all_to_all(
        jnp.broadcast_to(value[None], (length, *value.shape)), axis, 0, 0, tiled=True
    )


def over_copies(value, axis):
    return copy_for_each(value, axis).sum(axis=0)


def combine_levels(pieces, section_sum):
    levels = lax.axis_size("rep").bit_length() - 1
    own_index = lax.axis_index("rep")
    for section in range(levels):
        bit_pos = levels - 1 - section
        half_rows = pieces.shape[1] // 2
        upper_side = own_index >> bit_pos & 1
        kept_half = lax.dynamic_slice_in_dim(pieces, upper_side * half_rows, half_rows, 1)
        sent_half = lax.dynamic_slice_in_dim(pieces, (1 - upper_side) * half_rows, half_rows, 1)
        their_half = from_partner(sent_half, "rep", bit_pos)
        is_lower = upper_side == 0
        inner_own = jnp.sum(
            kept_half.astype(jnp.float32) * their_half.astype(jnp.float32), axis=(1, 2)
        )
        sq_kept = jnp.sum(jnp.square(kept_half.astype(jnp.float32)), axis=(1, 2))
        sq_their = jnp.sum(jnp.square(their_half.astype(jnp.float32)), axis=(1, 2))
        sq_first = jnp.where(is_lower, sq_kept, sq_their)
        sq_second = jnp.where(is_lower, sq_their, sq_kept)
        partial_stats = jnp.stack([inner_own, sq_first, sq_second], axis=1)
        totals = section_sum(partial_stats, bit_pos)
        coef_first = 1.0 - totals[:, 0] / (2.0 * (totals[:, 1] + tiny_eps))
        coef_second = 1.0 - totals[:, 0] / (2.0 * (totals[:, 2] + tiny_eps))
        coef_kept = jnp.where(is_lower, coef_first, coef_second)
        coef_their = jnp.where(is_lower, coef_second, coef_first)
        merged = coef_kept[:, None, None] * kept_half.astype(jnp.float32) + coef_their[
            :, None, None
        ] * their_half.astype(jnp.float32)
        if section == levels - 1:
            pieces = merged
        else:
            pieces = merged.astype(jnp.bfloat16)
    return pieces


def on_device(x_rows, row_cot, gate_vals, route_pos, weights, momentum):
    own_index = lax.axis_index("rep")

    def section_sum(partial_stats, bit_pos):
        groups = 1 << bit_pos
        group_id = own_index % groups
        onehot = (jnp.arange(groups, dtype=jnp.int32) == group_id).astype(jnp.float32)
        table = onehot[:, None, None] * partial_stats[None]
        summed = over_copies(table, "rep")
        return jnp.sum(onehot[:, None, None] * summed, axis=0)

    routed = x_rows[0]
    out_cot = row_cot[0]
    w_gate = weights[0, 0]
    w_up = weights[0, 1]
    w_down_t = weights[0, 2]
    contract_rows = (((0,), (0,)), ((), ()))
    contract_cols = (((1,), (1,)), ((), ()))
    gate_pre = jnp.dot(routed, w_gate, preferred_element_type=jnp.float32)
    up_pre = jnp.dot(routed, w_up, preferred_element_type=jnp.float32)
    sigma_gate = jax.nn.sigmoid(gate_pre)
    activation = gate_pre * sigma_gate
    hidden = (activation * up_pre).astype(jnp.bfloat16)
    scaled = (gate_vals[0][:, None] * out_cot.astype(jnp.float32)).astype(jnp.bfloat16)
    down_grad = lax.dot_general(scaled, hidden, contract_rows, preferred_element_type=jnp.float32)
    hidden_grad = jnp.dot(scaled, w_down_t, preferred_element_type=jnp.float32)
    gate_grad = (hidden_grad * up_pre * sigma_gate * (1.0 + gate_pre * (1.0 - sigma_gate))).astype(
        jnp.bfloat16
    )
    up_grad = (hidden_grad * activation).astype(jnp.bfloat16)
    row_grad = lax.dot_general(gate_grad, w_gate, contract_cols, preferred_element_type=jnp.float32)
    row_grad = row_grad + lax.dot_general(
        up_grad, w_up, contract_cols, preferred_element_type=jnp.float32
    )
    returned = lax.all_to_all(
        row_grad.astype(jnp.bfloat16), "exp", split_axis=0, concat_axis=0, tiled=True
    )
    picked = returned[route_pos[0]]
    token_grad = jnp.sum(picked.astype(jnp.float32), axis=1).astype(jnp.bfloat16)[None]
    grad_gate = lax.dot_general(
        routed, gate_grad, contract_rows, preferred_element_type=jnp.float32
    )
    grad_up = lax.dot_general(routed, up_grad, contract_rows, preferred_element_type=jnp.float32)
    grad_stack = jnp.stack(
        [
            grad_gate.astype(jnp.bfloat16),
            grad_up.astype(jnp.bfloat16),
            down_grad.astype(jnp.bfloat16),
        ],
        axis=0,
    )
    combined = combine_levels(grad_stack, section_sum)
    momentum_new = moment_decay * momentum + (1.0 - moment_decay) * combined[None]
    return (token_grad, momentum_new)


def solution(mesh):
    placed = (
        P("rep", "exp", None),
        P("rep", "exp", None),
        P("rep", "exp"),
        P("rep", "exp", None),
        P("exp", None, None, None),
        P("exp", None, "rep", None),
    )
    return jax.shard_map(
        on_device,
        mesh=mesh,
        in_specs=placed,
        out_specs=(P("rep", "exp", None), P("exp", None, "rep", None)),
        check_vma=False,
    )
```

profile of v0, /device:TPU:1, one launch (start us, length us, event | category | flops | bytes accessed | tf_op | source)
XLA Modules:
  0.0 412.9 jit_solution(12687813355468949499)
XLA Ops:
  16.4 7.9 %collective-permute-start = (bf16[3,1024,384]{1,2,0:T(8,128)(2,1)}, bf16[3,1024,384]{1,2,0:T(8,128)(2,1)S(1)}, u32[]{:S(2)}, u32[]{:S(2)}) collective-permute-start(bf16[3,1024,384]{1,2,0:T(8,128)(2,1)} %constant_dynamic-slice_fusion.5), channel_id=1, source_target_pairs={{0,512},{512,0},{16,528},{528,16},{32,544},{544,32},{48,560},{560,... | collective-permute-start | bytes 7077896 | tf_op jit(solution)/shard_map/ppermute | solution.py:17
  24.4 81.9 %collective-permute-done = bf16[3,1024,384]{1,2,0:T(8,128)(2,1)S(1)} collective-permute-done((bf16[3,1024,384]{1,2,0:T(8,128)(2,1)}, bf16[3,1024,384]{1,2,0:T(8,128)(2,1)S(1)}, u32[]{:S(2)}, u32[]{:S(2)}) %collective-permute-start) | collective-permute-done | bytes 2359328 | tf_op jit(solution)/shard_map/ppermute | solution.py:17
  106.3 4.2 %fusion.3 = (f32[3]{0:T(128)S(1)}, f32[3]{0:T(128)S(1)}, f32[3]{0:T(128)S(1)}) fusion(bf16[3,1024,384]{1,2,0:T(8,128)(2,1)S(1)} %collective-permute-done, bf16[3,2048,384]{1,2,0:T(8,128)(2,1)} %copy-done.1, s32[]{:T(128)S(6)} %select_n.365), kind=kLoop, calls=%fused_computation.9 | loop fusion | flops 9437175 | bytes 4718632 | tf_op jit(solution)/shard_map/reduce_sum | solution.py:42
  111.6 33.0 %all-to-all-start.1 = ((f32[64,1,288]{2,1,0:T(1,128)}), f32[64,1,288]{2,1,0:T(1,128)S(1)}, u32[]{:S(2)}, u32[]{:S(2)}) async-start(f32[64,1,288]{2,1,0:T(1,128)} %reshape.627), calls=%async_computation.1 | async-start | bytes 196608 | tf_op jit(solution)/shard_map/all_to_all | solution.py:22
  144.6 11.3 %all-to-all-done.1 = f32[64,1,288]{2,1,0:T(1,128)S(1)} async-done(((f32[64,1,288]{2,1,0:T(1,128)}), f32[64,1,288]{2,1,0:T(1,128)S(1)}, u32[]{:S(2)}, u32[]{:S(2)}) %all-to-all-start.1) | async-done | bytes 73760 | tf_op jit(solution)/shard_map/all_to_all | solution.py:22
  157.9 3.7 fusion.2
  165.3 53.5 %collective-permute-done.1 = bf16[3,512,384]{1,2,0:T(8,128)(2,1)} collective-permute-done((bf16[3,512,384]{1,2,0:T(8,128)(2,1)}, bf16[3,512,384]{1,2,0:T(8,128)(2,1)}, u32[]{:S(2)}, u32[]{:S(2)}) %collective-permute-start.1) | collective-permute-done | bytes 1179680 | tf_op jit(solution)/shard_map/ppermute | solution.py:17
  222.2 4.8 %all-to-all-start.2 = ((f32[64,1,144]{2,1,0:T(1,128)}), f32[64,1,144]{2,1,0:T(1,128)S(1)}, u32[]{:S(2)}, u32[]{:S(2)}) async-start(f32[64,1,144]{2,1,0:T(1,128)} %reshape.629), calls=%async_computation.2 | async-start | bytes 131072 | tf_op jit(solution)/shard_map/all_to_all | solution.py:22
  227.0 11.0 %all-to-all-done.2 = f32[64,1,144]{2,1,0:T(1,128)S(1)} async-done(((f32[64,1,144]{2,1,0:T(1,128)}), f32[64,1,144]{2,1,0:T(1,128)S(1)}, u32[]{:S(2)}, u32[]{:S(2)}) %all-to-all-start.2) | async-done | bytes 36896 | tf_op jit(solution)/shard_map/all_to_all | solution.py:22
  244.8 12.6 %collective-permute-done.2 = bf16[3,256,384]{1,2,0:T(8,128)(2,1)S(1)} collective-permute-done((bf16[3,256,384]{1,2,0:T(8,128)(2,1)S(1)}, bf16[3,256,384]{1,2,0:T(8,128)(2,1)S(1)}, u32[]{:S(2)}, u32[]{:S(2)}) %collective-permute-start.2) | collective-permute-done | bytes 589856 | tf_op jit(solution)/shard_map/ppermute | solution.py:17
  260.0 4.6 %all-to-all-start.3 = ((f32[64,8,3,3]{1,3,2,0:T(4,128)}), f32[64,8,3,3]{1,3,2,0:T(4,128)S(1)}, u32[]{:S(2)}, u32[]{:S(2)}) async-start(f32[64,8,3,3]{1,3,2,0:T(4,128)} %broadcast_in_dim.17), calls=%async_computation.3 | async-start | bytes 786432 | tf_op jit(solution)/shard_map/all_to_all | solution.py:22
  264.6 13.6 %all-to-all-done.3 = f32[64,8,3,3]{1,3,2,0:T(4,128)S(1)} async-done(((f32[64,8,3,3]{1,3,2,0:T(4,128)}), f32[64,8,3,3]{1,3,2,0:T(4,128)S(1)}, u32[]{:S(2)}, u32[]{:S(2)}) %all-to-all-start.3) | async-done | bytes 18464 | tf_op jit(solution)/shard_map/all_to_all | solution.py:22
  279.0 4.3 %collective-permute-start.3 = (bf16[3,128,384]{1,2,0:T(8,128)(2,1)S(1)}, bf16[3,128,384]{1,2,0:T(8,128)(2,1)S(1)}, u32[]{:S(2)}, u32[]{:S(2)}) collective-permute-start(bf16[3,128,384]{1,2,0:T(8,128)(2,1)S(1)} %constant_dynamic-slice_fusion.2), channel_id=1, source_target_pairs={{0,64},{64,0},{16,80},{80,16},{32,96},{96,32},{48,112},{112,48},{1... | collective-permute-start | bytes 884744 | tf_op jit(solution)/shard_map/ppermute | solution.py:17
  283.4 12.8 %collective-permute-done.3 = bf16[3,128,384]{1,2,0:T(8,128)(2,1)S(1)} collective-permute-done((bf16[3,128,384]{1,2,0:T(8,128)(2,1)S(1)}, bf16[3,128,384]{1,2,0:T(8,128)(2,1)S(1)}, u32[]{:S(2)}, u32[]{:S(2)}) %collective-permute-start.3) | collective-permute-done | bytes 294944 | tf_op jit(solution)/shard_map/ppermute | solution.py:17
  297.4 8.5 %all-to-all-start.4 = ((f32[64,4,3,3]{3,1,2,0:T(4,128)}), f32[64,4,3,3]{3,1,2,0:T(4,128)S(1)}, u32[]{:S(2)}, u32[]{:S(2)}) async-start(f32[64,4,3,3]{3,1,2,0:T(4,128)} %broadcast_in_dim.18), calls=%async_computation.4 | async-start | bytes 786432 | tf_op jit(solution)/shard_map/all_to_all | solution.py:22
  305.9 13.7 %all-to-all-done.4 = f32[64,4,3,3]{3,1,2,0:T(4,128)S(1)} async-done(((f32[64,4,3,3]{3,1,2,0:T(4,128)}), f32[64,4,3,3]{3,1,2,0:T(4,128)S(1)}, u32[]{:S(2)}, u32[]{:S(2)}) %all-to-all-start.4) | async-done | bytes 9248 | tf_op jit(solution)/shard_map/all_to_all | solution.py:22
  325.9 10.5 %collective-permute-done.4 = bf16[3,64,384]{1,2,0:T(8,128)(2,1)S(1)} collective-permute-done((bf16[3,64,384]{1,2,0:T(8,128)(2,1)S(1)}, bf16[3,64,384]{1,2,0:T(8,128)(2,1)S(1)}, u32[]{:S(2)}, u32[]{:S(2)}) %collective-permute-start.4) | collective-permute-done | bytes 147488 | tf_op jit(solution)/shard_map/ppermute | solution.py:17
  337.7 8.2 %all-to-all-start.5 = ((f32[64,2,3,3]{3,1,2,0:T(2,128)}), f32[64,2,3,3]{3,1,2,0:T(2,128)S(1)}, u32[]{:S(2)}, u32[]{:S(2)}) async-start(f32[64,2,3,3]{3,1,2,0:T(2,128)} %broadcast_in_dim.19), calls=%async_computation.5 | async-start | bytes 393216 | tf_op jit(solution)/shard_map/all_to_all | solution.py:22
  348.8 9.1 %all-to-all-done.5 = f32[64,2,3,3]{3,1,2,0:T(2,128)S(1)} async-done(((f32[64,2,3,3]{3,1,2,0:T(2,128)}), f32[64,2,3,3]{3,1,2,0:T(2,128)S(1)}, u32[]{:S(2)}, u32[]{:S(2)}) %all-to-all-start.5) | async-done | bytes 4640 | tf_op jit(solution)/shard_map/all_to_all | solution.py:22
  357.8 19.3 %all-to-all-start = ((bf16[16,8,2048]{2,1,0:T(8,128)(2,1)}), bf16[16,8,2048]{2,1,0:T(8,128)(2,1)S(1)}, u32[]{:S(2)}, u32[]{:S(2)}) async-start(bf16[16,8,2048]{2,1,0:T(8,128)(2,1)} %fusion.14), calls=%async_computation | async-start | bytes 1048576 | tf_op jit(solution)/shard_map/all_to_all | solution.py:99
  380.5 7.9 %collective-permute-done.5 = bf16[3,32,384]{1,2,0:T(8,128)(2,1)S(1)} collective-permute-done((bf16[3,32,384]{1,2,0:T(8,128)(2,1)S(1)}, bf16[3,32,384]{1,2,0:T(8,128)(2,1)S(1)}, u32[]{:S(2)}, u32[]{:S(2)}) %collective-permute-start.5) | collective-permute-done | bytes 73760 | tf_op jit(solution)/shard_map/ppermute | solution.py:17
  388.9 5.6 %all-to-all-done = bf16[16,8,2048]{2,1,0:T(8,128)(2,1)S(1)} async-done(((bf16[16,8,2048]{2,1,0:T(8,128)(2,1)}), bf16[16,8,2048]{2,1,0:T(8,128)(2,1)S(1)}, u32[]{:S(2)}, u32[]{:S(2)}) %all-to-all-start) | async-done | bytes 524320 | tf_op jit(solution)/shard_map/all_to_all | solution.py:99
  395.1 4.6 %all-to-all-start.6 = ((f32[64,1,3,3]{3,1,2,0:T(1,128)}), f32[64,1,3,3]{3,1,2,0:T(1,128)S(1)}, u32[]{:S(2)}, u32[]{:S(2)}) async-start(f32[64,1,3,3]{3,1,2,0:T(1,128)} %broadcast_in_dim.20), calls=%async_computation.6 | async-start | bytes 196608 | tf_op jit(solution)/shard_map/all_to_all | solution.py:22
  402.0 9.4 %all-to-all-done.6 = f32[64,1,3,3]{3,1,2,0:T(1,128)S(1)} async-done(((f32[64,1,3,3]{3,1,2,0:T(1,128)}), f32[64,1,3,3]{3,1,2,0:T(1,128)S(1)}, u32[]{:S(2)}, u32[]{:S(2)}) %all-to-all-start.6) | async-done | bytes 2336 | tf_op jit(solution)/shard_map/all_to_all | solution.py:22
  (120 shorter events, 55.8 us)
Async XLA Ops:
  0.6 1.0 copy-start
  0.6 4.7 %copy-start.5 = (bf16[1,128,2048]{2,1,0:T(8,128)(2,1)S(1)}, bf16[1,128,2048]{2,1,0:T(8,128)(2,1)}, u32[]{:S(2)}) copy-start(bf16[1,128,2048]{2,1,0:T(8,128)(2,1)} %param.7) | copy-start | bytes 1572868
  0.7 4.7 %copy-start.8 = (f32[1,128]{1,0:T(1,128)S(1)}, f32[1,128]{1,0:T(1,128)}, u32[]{:S(2)}) copy-start(f32[1,128]{1,0:T(1,128)} %param.8) | copy-start | bytes 1540
  13.6 2.8 copy-start.1
  16.4 89.8 %collective-permute-start = (bf16[3,1024,384]{1,2,0:T(8,128)(2,1)}, bf16[3,1024,384]{1,2,0:T(8,128)(2,1)S(1)}, u32[]{:S(2)}, u32[]{:S(2)}) collective-permute-start(bf16[3,1024,384]{1,2,0:T(8,128)(2,1)} %constant_dynamic-slice_fusion.5), channel_id=1, source_target_pairs={{0,512},{512,0},{16,528},{528,16},{32,544},{544,32},{48,560},{560,... | collective-permute-start | bytes 7077896 | tf_op jit(solution)/shard_map/ppermute | solution.py:17
  106.3 4.2 %copy-start.2 = (bf16[3,1024,384]{1,2,0:T(8,128)(2,1)}, bf16[3,1024,384]{1,2,0:T(8,128)(2,1)S(1)}, u32[]{:S(2)}) copy-start(bf16[3,1024,384]{1,2,0:T(8,128)(2,1)S(1)} %collective-permute-done) | copy-start | bytes 7077892
  111.6 44.3 %all-to-all-start.1 = ((f32[64,1,288]{2,1,0:T(1,128)}), f32[64,1,288]{2,1,0:T(1,128)S(1)}, u32[]{:S(2)}, u32[]{:S(2)}) async-start(f32[64,1,288]{2,1,0:T(1,128)} %reshape.627), calls=%async_computation.1 | async-start | bytes 196608 | tf_op jit(solution)/shard_map/all_to_all | solution.py:22
  162.8 56.0 %collective-permute-start.1 = (bf16[3,512,384]{1,2,0:T(8,128)(2,1)}, bf16[3,512,384]{1,2,0:T(8,128)(2,1)}, u32[]{:S(2)}, u32[]{:S(2)}) collective-permute-start(bf16[3,512,384]{1,2,0:T(8,128)(2,1)} %constant_dynamic-slice_fusion.4), channel_id=1, source_target_pairs={{0,256},{256,0},{16,272},{272,16},{32,288},{288,32},{48,304},{304,... | collective-permute-start | bytes 3538952 | tf_op jit(solution)/shard_map/ppermute | solution.py:17
  222.2 15.8 %all-to-all-start.2 = ((f32[64,1,144]{2,1,0:T(1,128)}), f32[64,1,144]{2,1,0:T(1,128)S(1)}, u32[]{:S(2)}, u32[]{:S(2)}) async-start(f32[64,1,144]{2,1,0:T(1,128)} %reshape.629), calls=%async_computation.2 | async-start | bytes 131072 | tf_op jit(solution)/shard_map/all_to_all | solution.py:22
  241.3 1.0 copy-start.3
  242.4 36.3 %copy-start.4 = (bf16[3,512,384]{1,2,0:T(8,128)(2,1)S(1)}, bf16[3,512,384]{1,2,0:T(8,128)(2,1)}, u32[]{:S(2)}) copy-start(bf16[3,512,384]{1,2,0:T(8,128)(2,1)} %copy-done.3) | copy-start | bytes 3538948
  242.4 15.0 %collective-permute-start.2 = (bf16[3,256,384]{1,2,0:T(8,128)(2,1)S(1)}, bf16[3,256,384]{1,2,0:T(8,128)(2,1)S(1)}, u32[]{:S(2)}, u32[]{:S(2)}) collective-permute-start(bf16[3,256,384]{1,2,0:T(8,128)(2,1)S(1)} %constant_dynamic-slice_fusion.3), channel_id=1, source_target_pairs={{0,128},{128,0},{16,144},{144,16},{32,160},{160,32},{48,176},{176,... | collective-permute-start | bytes 1769480 | tf_op jit(solution)/shard_map/ppermute | solution.py:17
  260.0 18.2 %all-to-all-start.3 = ((f32[64,8,3,3]{1,3,2,0:T(4,128)}), f32[64,8,3,3]{1,3,2,0:T(4,128)S(1)}, u32[]{:S(2)}, u32[]{:S(2)}) async-start(f32[64,8,3,3]{1,3,2,0:T(4,128)} %broadcast_in_dim.17), calls=%async_computation.3 | async-start | bytes 786432 | tf_op jit(solution)/shard_map/all_to_all | solution.py:22
  279.0 17.1 %collective-permute-start.3 = (bf16[3,128,384]{1,2,0:T(8,128)(2,1)S(1)}, bf16[3,128,384]{1,2,0:T(8,128)(2,1)S(1)}, u32[]{:S(2)}, u32[]{:S(2)}) collective-permute-start(bf16[3,128,384]{1,2,0:T(8,128)(2,1)S(1)} %constant_dynamic-slice_fusion.2), channel_id=1, source_target_pairs={{0,64},{64,0},{16,80},{80,16},{32,96},{96,32},{48,112},{112,48},{1... | collective-permute-start | bytes 884744 | tf_op jit(solution)/shard_map/ppermute | solution.py:17
  297.4 22.1 %all-to-all-start.4 = ((f32[64,4,3,3]{3,1,2,0:T(4,128)}), f32[64,4,3,3]{3,1,2,0:T(4,128)S(1)}, u32[]{:S(2)}, u32[]{:S(2)}) async-start(f32[64,4,3,3]{3,1,2,0:T(4,128)} %broadcast_in_dim.18), calls=%async_computation.4 | async-start | bytes 786432 | tf_op jit(solution)/shard_map/all_to_all | solution.py:22
  320.4 16.1 %collective-permute-start.4 = (bf16[3,64,384]{1,2,0:T(8,128)(2,1)S(1)}, bf16[3,64,384]{1,2,0:T(8,128)(2,1)S(1)}, u32[]{:S(2)}, u32[]{:S(2)}) collective-permute-start(bf16[3,64,384]{1,2,0:T(8,128)(2,1)S(1)} %constant_dynamic-slice_fusion.1), channel_id=1, source_target_pairs={{0,32},{32,0},{16,48},{48,16},{64,96},{96,64},{80,112},{112,80},{1... | collective-permute-start | bytes 442376 | tf_op jit(solution)/shard_map/ppermute | solution.py:17
  337.7 20.1 %all-to-all-start.5 = ((f32[64,2,3,3]{3,1,2,0:T(2,128)}), f32[64,2,3,3]{3,1,2,0:T(2,128)S(1)}, u32[]{:S(2)}, u32[]{:S(2)}) async-start(f32[64,2,3,3]{3,1,2,0:T(2,128)} %broadcast_in_dim.19), calls=%async_computation.5 | async-start | bytes 393216 | tf_op jit(solution)/shard_map/all_to_all | solution.py:22
  345.9 34.3 %copy-start.7 = (s32[1,20,4]{1,2,0:T(4,128)S(1)}, s32[1,20,4]{1,2,0:T(4,128)}, u32[]{:S(2)}) copy-start(s32[1,20,4]{1,2,0:T(4,128)} %param.9) | copy-start | bytes 964
  348.8 51.0 %copy-start.6 = (f32[1,3,32,384]{3,2,1,0:T(8,128)S(1)}, f32[1,3,32,384]{3,2,1,0:T(8,128)}, u32[]{:S(2)}) copy-start(f32[1,3,32,384]{3,2,1,0:T(8,128)} %param.11) | copy-start | bytes 442372
  357.8 36.6 %all-to-all-start = ((bf16[16,8,2048]{2,1,0:T(8,128)(2,1)}), bf16[16,8,2048]{2,1,0:T(8,128)(2,1)S(1)}, u32[]{:S(2)}, u32[]{:S(2)}) async-start(bf16[16,8,2048]{2,1,0:T(8,128)(2,1)} %fusion.14), calls=%async_computation | async-start | bytes 1048576 | tf_op jit(solution)/shard_map/all_to_all | solution.py:99
  377.9 10.5 %collective-permute-start.5 = (bf16[3,32,384]{1,2,0:T(8,128)(2,1)S(1)}, bf16[3,32,384]{1,2,0:T(8,128)(2,1)S(1)}, u32[]{:S(2)}, u32[]{:S(2)}) collective-permute-start(bf16[3,32,384]{1,2,0:T(8,128)(2,1)S(1)} %constant_dynamic-slice_fusion), channel_id=1, source_target_pairs={{0,16},{16,0},{32,48},{48,32},{64,80},{80,64},{96,112},{112,96},{1... | collective-permute-start | bytes 221192 | tf_op jit(solution)/shard_map/ppermute | solution.py:17
  395.1 16.3 %all-to-all-start.6 = ((f32[64,1,3,3]{3,1,2,0:T(1,128)}), f32[64,1,3,3]{3,1,2,0:T(1,128)S(1)}, u32[]{:S(2)}, u32[]{:S(2)}) async-start(f32[64,1,3,3]{3,1,2,0:T(1,128)} %broadcast_in_dim.20), calls=%async_computation.6 | async-start | bytes 196608 | tf_op jit(solution)/shard_map/all_to_all | solution.py:22
where the time goes:
time: 414 us; the launch traced here: 413 us
  waiting for transfers between devices  253 us (61%)
  starting transfers between devices  106 us (26%)
  other arithmetic  23.4 us (6%)
  local copies, waits for them, and re-layouts  15.1 us (4%)
  matrix products  14.6 us (4%)
    ppermute x6, waiting for transfers between devices, from_partner(): return lax.ppermute(block, axis, route)  179 us
    all_to_all x6, waiting for transfers between devices, copy_for_each(): lax.all_to_all(jnp.broadcast_to(value[None], (length, *value.shape)), axi...  67.9 us
    all_to_all x6, starting transfers between devices, copy_for_each(): lax.all_to_all(jnp.broadcast_to(value[None], (length, *value.shape)), axi...  63.7 us
    ppermute x6, starting transfers between devices, from_partner(): return lax.ppermute(block, axis, route)  22.9 us
    all_to_all x1, starting transfers between devices, on_device(): lax.all_to_all(row_grad.astype(jnp.bfloat16), 'exp', split_axis=0, concat...  19.3 us
    reduce_sum x6, other arithmetic, combine_levels(): jnp.sum(kept_half.astype(jnp.float32) * their_half.astype(jnp.float32), a...  8.9 us
  transfers between devices with their start and end apart: 13, of which 13 were waited for; matrix products, arithmetic and copies ran while one was open for 2% of the time, Pallas kernels for 0%

commit v1 on v0

v1 whole, which is shorter than its diff:
```python
import functools
import math

import jax
import jax.numpy as jnp
from jax import lax
from jax.experimental import pallas as pl
from jax.experimental.pallas import tpu as pltpu
from jax.sharding import PartitionSpec as P

MESH = pl.DeviceIdType.MESH
tiny_eps = 1e-06
moment_decay = 0.9
ROWS_FIRST = (((0,), (0,)), ((), ()))
COLS_LAST = (((1,), (1,)), ((), ()))
f32 = jnp.float32
bf16 = jnp.bfloat16


def tile_iotas():
    sub = lax.broadcasted_iota(jnp.int32, (8, 128), 0)
    lane = lax.broadcasted_iota(jnp.int32, (8, 128), 1)
    return sub, lane


def gram_tile(read, n, rows, cols, rows_buf):
    pairs = [(k, l) for k in range(n) for l in range(k, n)]

    def body(i, accs):
        row = pl.multiple_of(i * 8, 8)
        accs = list(accs)
        for c in range(cols // 128):
            vals = [read(k, row, c * 128) for k in range(n)]
            for at, (k, l) in enumerate(pairs):
                accs[at] = accs[at] + vals[k] * vals[l]
        return tuple(accs)

    zero = jnp.zeros((8, 128), f32)
    accs = lax.fori_loop(0, rows // 8, body, tuple(zero for _ in pairs))
    for (k, l), acc in zip(pairs, accs):
        total = jnp.sum(acc, axis=0, keepdims=True)
        for a in range(8):
            for b in range(8):
                if sorted((a % n, b % n)) == [k, l]:
                    rows_buf[a * 8 + b : a * 8 + b + 1, :] = total
    sub, lane = tile_iotas()
    tile = zero
    for b in range(8):
        col = jnp.sum(rows_buf[b * 8 : b * 8 + 8, :], axis=1, keepdims=True)
        tile = tile + jnp.where((lane & 7) == b, col, 0.0)
    return tile


def tree_weights(tile, n):
    sub, lane = tile_iotas()
    weights = jnp.ones((8, 128), f32)
    half = n // 2
    while half >= 1:
        other = (sub + half) & 7
        here_c = jnp.where(lane == sub, tile, 0.0)
        there_c = jnp.where(lane == other, tile, 0.0)
        here_r = jnp.where((lane & 7) == sub, tile, 0.0)
        there_r = jnp.where((lane & 7) == other, tile, 0.0)
        q_col = jnp.maximum(jnp.sum(here_c, axis=1, keepdims=True), 0.0)
        p_col = jnp.sum(there_c, axis=1, keepdims=True)
        q_row = jnp.maximum(jnp.sum(here_r, axis=0, keepdims=True), 0.0)
        p_row = jnp.sum(there_r, axis=0, keepdims=True)
        q_col_b = jnp.broadcast_to(q_col, (8, 128))
        q_row_b = jnp.broadcast_to(q_row, (8, 128))
        most_c = jnp.sqrt(q_col_b) * jnp.sqrt(pltpu.roll(q_col_b, half, 0))
        most_r = jnp.sqrt(q_row_b) * jnp.sqrt(pltpu.roll(q_row_b, half, 1))
        p_col_b = jnp.clip(jnp.broadcast_to(p_col, (8, 128)), -most_c, most_c)
        p_row_b = jnp.clip(jnp.broadcast_to(p_row, (8, 128)), -most_r, most_r)
        coef_c = 1.0 - p_col_b / (2.0 * (q_col_b + tiny_eps))
        coef_r = 1.0 - p_row_b / (2.0 * (q_row_b + tiny_eps))
        weights = weights * coef_c
        tile = tile * coef_c * coef_r
        tile = tile + pltpu.roll(tile, half, 0)
        tile = tile + pltpu.roll(tile, half, 1)
        half //= 2
    return weights


def summed_tiles(buf, n, shifted):
    total = buf[0]
    for j in range(1, n):
        tile = buf[j]
        if shifted:
            tile = pltpu.roll(pltpu.roll(tile, j, 0), j, 1)
        total = total + tile
    return total


def kernel(
    nx, ny, ne,
    x_ref, cot_ref, gate_ref, route_ref, w_ref,
    token_ref, comb_ref,
    cot_v, w_v, xs, ss, xr, sr, a_buf, g_buf, zs, zr,
    c3, yr, yf, st1, st2, st3, rows_buf, wt_buf,
    load_sem, x_sem, xsend, xrecv, asend, arecv, zsend, zrecv,
    ysend, yrecv, s1send, s1recv, s2send, s2recv, s3send, s3recv,
):
    rep = lax.axis_index("rep")
    me_e = lax.axis_index("exp")
    me_x = lax.div(rep, ny)
    me_y = lax.rem(rep, ny)
    rows, width = cot_v.shape
    ff = w_v.shape[2]
    dx = width // nx
    dy = dx // ny
    half_w = width // 2

    def x_peer(k):
        return (lax.rem(me_x + k, nx) * ny + me_y, me_e)

    def y_peer(k):
        return (me_x * ny + lax.rem(me_y + k, ny), me_e)

    def e_peer(k):
        return (rep, lax.rem(me_e + k, ne))

    cot_load = pltpu.make_async_copy(cot_ref.at[0], cot_v, load_sem.at[0])
    cot_load.start()
    x_loads = []
    for j in range(nx):
        load = pltpu.make_async_copy(x_ref.at[0, :, pl.ds(j * dx, dx)], xs.at[j], x_sem.at[j])
        load.start()
        x_loads.append(load)
    w_loads = []
    for t in range(3):
        load = pltpu.make_async_copy(w_ref.at[0, t], w_v.at[t], load_sem.at[1 + t])
        load.start()
        w_loads.append(load)

    barrier = pltpu.get_barrier_semaphore()
    peers = [x_peer(k) for k in range(1, nx)]
    peers += [y_peer(k) for k in range(1, ny)]
    peers += [e_peer(k) for k in range(1, ne)]
    for peer in peers:
        pl.semaphore_signal(barrier, inc=1, device_id=peer, device_id_type=MESH)

    eye = lax.broadcasted_iota(jnp.int32, (rows, rows), 0) == lax.broadcasted_iota(
        jnp.int32, (rows, rows), 1
    )
    gate_col = jnp.sum(jnp.where(eye, gate_ref[...], 0.0), axis=1, keepdims=True)
    cot_load.wait()
    for j in range(nx):
        ss[j] = (gate_col * cot_v[:, j * dx : (j + 1) * dx].astype(f32)).astype(bf16)

    if peers:
        pl.semaphore_wait(barrier, len(peers))

    def send(src, dst, ssem, rsem, peer):
        copy = pltpu.make_async_remote_copy(
            src_ref=src, dst_ref=dst, send_sem=ssem, recv_sem=rsem,
            device_id=peer, device_id_type=MESH,
        )
        copy.start()

    def wait_bytes(ref, sem):
        pltpu.make_async_copy(ref, ref, sem).wait()

    order_x = sorted(range(1, nx), key=lambda k: -min(k, nx - k))
    order_y = sorted(range(1, ny), key=lambda k: -min(k, ny - k))

    for k in order_x:
        send(ss.at[lax.rem(me_x + k, nx)], sr.at[nx - k], xsend.at[0], xrecv.at[0], x_peer(k))
    sr[0] = ss[me_x]
    for load in x_loads:
        load.wait()
    for k in order_x:
        send(xs.at[lax.rem(me_x + k, nx)], xr.at[nx - k], xsend.at[1], xrecv.at[1], x_peer(k))
    xr[0] = xs[me_x]

    far = nx // 2

    def ring_parts(step):
        parts = []
        if step < far:
            parts.append(((nx - step + 1) % nx, nx - step, 0, rows, 1))
            parts.append((step - 1, step, 0, rows, nx - 1))
        else:
            parts.append(((nx - step + 1) % nx, far, 0, rows // 2, 1))
            parts.append((step - 1, far, rows // 2, rows // 2, nx - 1))
        return parts

    def ring_refs(t, step):
        found = []
        for way, (src, dst, first, count, offset) in enumerate(ring_parts(step)):
            found.append((
                a_buf.at[t, src, pl.ds(first, count)],
                a_buf.at[t, dst, pl.ds(first, count)],
                (t * far + step - 1) * 2 + way,
                offset,
            ))
        return found

    def ring_wait(t, step):
        for src, dst, at, offset in ring_refs(t, step):
            wait_bytes(dst, arecv.at[at])

    def ring_step(t, step):
        if step > 1:
            ring_wait(t, step - 1)
        for src, dst, at, offset in ring_refs(t, step):
            send(src, dst, asend.at[at], arecv.at[at], x_peer(offset))

    w_loads[0].wait()
    w_loads[1].wait()
    gate_pre = jnp.zeros((rows, ff), f32)
    up_pre = jnp.zeros((rows, ff), f32)
    for j in range(nx):
        part = xs[j]
        gate_pre += jnp.dot(part, w_v[0, j * dx : (j + 1) * dx, :], preferred_element_type=f32)
        up_pre += jnp.dot(part, w_v[1, j * dx : (j + 1) * dx, :], preferred_element_type=f32)
    sigma = 1.0 / (1.0 + jnp.exp(-gate_pre))
    act = gate_pre * sigma
    a_buf[0, 0] = (act * up_pre).astype(bf16)
    ring_step(0, 1)

    w_loads[2].wait()
    hidden_grad = jnp.zeros((rows, ff), f32)
    for j in range(nx):
        hidden_grad += jnp.dot(ss[j], w_v[2, j * dx : (j + 1) * dx, :], preferred_element_type=f32)
    a_buf[1, 0] = (hidden_grad * up_pre * sigma * (1.0 + gate_pre * (1.0 - sigma))).astype(bf16)
    ring_step(1, 1)
    a_buf[2, 0] = (hidden_grad * act).astype(bf16)
    ring_step(2, 1)

    def row_grads():
        gate_grad = a_buf[1, 0]
        up_grad = a_buf[2, 0]
        blk = min(256, half_w)

        def piece(col):
            at = pl.ds(pl.multiple_of(col, blk), blk)
            val = lax.dot_general(gate_grad, w_v[0, at, :], COLS_LAST, preferred_element_type=f32)
            val += lax.dot_general(up_grad, w_v[1, at, :], COLS_LAST, preferred_element_type=f32)
            return val.reshape(ne, rows // ne, blk)

        def body(j, carry):
            both = jnp.concatenate([piece(j * blk), piece(half_w + j * blk)], axis=1)
            zs[:, :, pl.ds(pl.multiple_of(j * blk, blk), blk)] = both.astype(bf16)
            return carry

        lax.fori_loop(0, half_w // blk, body, 0)
        for k in range(1, ne):
            send(zs.at[lax.rem(me_e + k, ne)], zr.at[ne - k], zsend.at[0], zrecv.at[0], e_peer(k))
        zr[0] = zs[me_e]

    def tokens():
        wait_bytes(zr.at[pl.ds(1, ne - 1)], zrecv.at[0])
        cap = rows // ne
        tall = ne * 2 * cap
        count = token_ref.shape[1]
        route = route_ref[0]
        at = ((lax.div(route, cap) - me_e + ne) & (ne - 1)) * (2 * cap) + lax.rem(route, cap)
        col = lax.broadcasted_iota(jnp.int32, (count, tall), 1)
        low = jnp.zeros((count, tall), f32)
        high = jnp.zeros((count, tall), f32)
        for k in range(route.shape[1]):
            low += jnp.where(col == at[:, k : k + 1], 1.0, 0.0)
            high += jnp.where(col == at[:, k : k + 1] + cap, 1.0, 0.0)
        got = zr[...].reshape(tall, half_w)
        token_ref[0, :, :half_w] = jnp.dot(low.astype(bf16), got, preferred_element_type=f32)
        token_ref[0, :, half_w:] = jnp.dot(high.astype(bf16), got, preferred_element_type=f32)

    def combine_1(t):
        left = sr if t == 0 else xr

        def body(k, carry):
            g_buf[t, k] = lax.dot_general(left[k], a_buf[t, k], ROWS_FIRST, preferred_element_type=f32)
            return carry

        lax.fori_loop(0, nx, body, 0)

        def read(k, row, col):
            return g_buf[t, k, pl.ds(row, 8), col : col + 128]

        st1[t, 0] = gram_tile(read, nx, dx, ff, rows_buf)
        for k in order_x:
            send(st1.at[t, 0], st1.at[t, nx - k], s1send.at[t], s1recv.at[t], x_peer(k))

    def combine_2(t):
        wait_bytes(st1.at[t, pl.ds(1, nx - 1)], s1recv.at[t])
        wt_buf[...] = tree_weights(summed_tiles(st1.at[t], nx, True), nx)
        lanes = [wt_buf[k : k + 1, :] for k in range(nx)]

        def body(i, carry):
            at = pl.ds(pl.multiple_of(i * 16, 16), 16)
            for c in range(ff // 128):
                cols = slice(c * 128, c * 128 + 128)
                total = lanes[0] * g_buf[t, 0, at, cols]
                for k in range(1, nx):
                    total = total + lanes[k] * g_buf[t, k, at, cols]
                c3[t, at, cols] = total.astype(bf16)
            return carry

        lax.fori_loop(0, dx // 16, body, 0)
        for k in order_y:
            first = pl.multiple_of(lax.rem(me_y + k, ny) * dy, dy)
            send(c3.at[t, pl.ds(first, dy)], yr.at[t, ny - k], ysend.at[t], yrecv.at[t], y_peer(k))
        yr[t, 0] = c3[t, pl.ds(pl.multiple_of(me_y * dy, dy), dy)]

    def combine_3(t):
        wait_bytes(yr.at[t, pl.ds(1, ny - 1)], yrecv.at[t])
        yf[t] = yr[t].astype(f32)

        def read(k, row, col):
            return yf[t, k, pl.ds(row, 8), col : col + 128]

        st2[t, 0] = gram_tile(read, ny, dy, ff, rows_buf)
        for k in order_x:
            send(st2.at[t, 0], st2.at[t, nx - k], s2send.at[t], s2recv.at[t], x_peer(k))

    def combine_4(t):
        wait_bytes(st2.at[t, pl.ds(1, nx - 1)], s2recv.at[t])
        st3[t, 0] = summed_tiles(st2.at[t], nx, False)
        for k in order_y:
            send(st3.at[t, 0], st3.at[t, ny - k], s3send.at[t], s3recv.at[t], y_peer(k))

    def combine_5(t):
        wait_bytes(st3.at[t, pl.ds(1, ny - 1)], s3recv.at[t])
        wt_buf[...] = tree_weights(summed_tiles(st3.at[t], ny, True), ny)
        for c in range(ff // 128):
            cols = slice(c * 128, c * 128 + 128)
            total = wt_buf[0:1, :] * yf[t, 0, :, cols]
            for k in range(1, ny):
                total = total + wt_buf[k : k + 1, :] * yf[t, k, :, cols]
            comb_ref[(t + 2) % 3, :, cols] = total

    def ready(t):
        ring_wait(t, far)
        if t < 2:
            wait_bytes((sr, xr)[t].at[pl.ds(1, nx - 1)], xrecv.at[t])

    ring_step(0, 2)
    row_grads()
    for step in range(2, far + 1):
        for t in range(3):
            if (t, step) != (0, 2):
                ring_step(t, step)
    tokens()
    ready(0)
    combine_1(0)
    ready(1)
    combine_1(1)
    combine_2(0)
    ready(2)
    combine_1(2)
    combine_2(1)
    combine_3(0)
    combine_2(2)
    combine_3(1)
    combine_4(0)
    combine_3(2)
    combine_4(1)
    combine_5(0)
    combine_4(2)
    combine_5(1)
    combine_5(2)

    for t, ref in enumerate((sr, xr)):
        wait_bytes(ref.at[pl.ds(1, nx - 1)], xsend.at[t])
    for t in range(3):
        for step in range(1, far + 1):
            for src, dst, at, offset in ring_refs(t, step):
                wait_bytes(src, asend.at[at])
        wait_bytes(st1.at[t, pl.ds(1, nx - 1)], s1send.at[t])
        wait_bytes(yr.at[t, pl.ds(1, ny - 1)], ysend.at[t])
        wait_bytes(st2.at[t, pl.ds(1, nx - 1)], s2send.at[t])
        wait_bytes(st3.at[t, pl.ds(1, ny - 1)], s3send.at[t])
    wait_bytes(zr.at[pl.ds(1, ne - 1)], zsend.at[0])


def on_device(nx, ny, ne, x_rows, row_cot, gate_vals, route_pos, weights, momentum):
    rows, width = x_rows.shape[1:]
    ff = weights.shape[3]
    dx = width // nx
    dy = dx // ny
    far = nx // 2
    tokens = route_pos.shape[1]
    vmem = pltpu.VMEM
    dma = pltpu.SemaphoreType.DMA
    in_hbm = pl.BlockSpec(memory_space=pl.ANY)
    in_vmem = pl.BlockSpec(memory_space=pltpu.VMEM)
    token_sum, combined = pl.pallas_call(
        functools.partial(kernel, nx, ny, ne),
        out_shape=(
            jax.ShapeDtypeStruct((1, tokens, width), f32),
            jax.ShapeDtypeStruct((3, dy, ff), f32),
        ),
        in_specs=[in_hbm, in_hbm, in_vmem, in_vmem, in_hbm],
        out_specs=(in_vmem, in_vmem),
        scratch_shapes=[
            vmem((rows, width), bf16),
            vmem((3, width, ff), bf16),
            vmem((nx, rows, dx), bf16),
            vmem((nx, rows, dx), bf16),
            vmem((nx, rows, dx), bf16),
            vmem((nx, rows, dx), bf16),
            vmem((3, nx, rows, ff), bf16),
            vmem((3, nx, dx, ff), f32),
            vmem((ne, 2 * rows // ne, width // 2), bf16),
            vmem((ne, 2 * rows // ne, width // 2), bf16),
            vmem((3, dx, ff), bf16),
            vmem((3, ny, dy, ff), bf16),
            vmem((3, ny, dy, ff), f32),
            vmem((3, nx, 8, 128), f32),
            vmem((3, nx, 8, 128), f32),
            vmem((3, ny, 8, 128), f32),
            vmem((64, 128), f32),
            vmem((8, 128), f32),
            dma((4,)),
            dma((nx,)),
            dma((2,)),
            dma((2,)),
            dma((6 * far,)),
            dma((6 * far,)),
            dma((1,)),
            dma((1,)),
            dma((3,)),
            dma((3,)),
            dma((3,)),
            dma((3,)),
            dma((3,)),
            dma((3,)),
            dma((3,)),
            dma((3,)),
        ],
        compiler_params=pltpu.CompilerParams(
            collective_id=0, has_side_effects=True, vmem_limit_bytes=56 * 1024 * 1024
        ),
        cost_estimate=pl.CostEstimate(
            flops=16 * rows * width * ff, bytes_accessed=2 * (3 * width * ff + 2 * rows * width),
            transcendentals=rows * ff,
        ),
    )(x_rows, row_cot, gate_vals, route_pos, weights)
    token_grad = token_sum.astype(bf16)
    momentum_new = moment_decay * momentum + (1.0 - moment_decay) * combined[None]
    return (token_grad, momentum_new)


def solution(mesh):
    reps, ne = mesh.shape["rep"], mesh.shape["exp"]
    nx = 1 << ((reps.bit_length()) // 2)
    ny = reps // nx
    placed = (
        P("rep", "exp", None),
        P("rep", "exp", None),
        P("rep", "exp"),
        P("rep", "exp", None),
        P("exp", None, None, None),
        P("exp", None, "rep", None),
    )
    return jax.shard_map(
        functools.partial(on_device, nx, ny, ne),
        mesh=mesh,
        in_specs=placed,
        out_specs=(P("rep", "exp", None), P("exp", None, "rep", None)),
        check_vma=False,
    )
```

time: 414 us -> 107 us (0.26)
  the two profiles are of different devices: /device:TPU:1 before, /device:TPU:2 now
where the time goes in v1:
time: 107 us; the launch traced here: 106 us
  Pallas kernels  101 us (94%)
  other arithmetic  3.17 us (3%)
  local copies, waits for them, and re-layouts  1.41 us (1%)
    pallas_call x1, Pallas kernels, on_device(): pl.pallas_call(functools.partial(kernel, nx, ny, ne), out_shape=(jax.Shap...  101 us

profile of v1, /device:TPU:2, one launch (start us, length us, event | category | flops | bytes accessed | tf_op | source)
XLA Modules:
  0.0 106.4 jit_solution(3111453130691174181)
XLA Ops:
  0.6 0.0 copy-start
  0.6 1.4 %copy.8.route_ref = s32[1,20,4]{2,1,0:T(8,128)} copy(s32[1,20,4]{1,2,0:T(4,128)} %param.9) | data formatting | bytes 640 | tf_op args[3]
  2.0 101.2 %shard_map.77 = (f32[1,20,2048]{2,1,0:T(8,128)}, f32[3,32,384]{2,1,0:T(8,128)}) custom-call(bf16[1,128,2048]{2,1,0:T(8,128)(2,1)} %x_ref.1, bf16[1,128,2048]{2,1,0:T(8,128)(2,1)} %cot_ref.1, f32[1,128]{1,0:T(1,128)} %gate_ref.1, s32[1,20,4]{2,1,0:T(8,128)} %copy.8.route_ref, bf16[1,3,2048,384]{3,2,1,0:T(8,128)(2,1)} %w_ref.1), custom_call_target="tpu_custom_call" | custom-call | flops 1610612736 | bytes 5767168 | tf_op jit(solution)/shard_map/pallas_call | solution.py:387
  103.2 1.6 %convert_element_type.3 = bf16[1,20,2048]{2,1,0:T(8,128)(2,1)} convert(f32[1,20,2048]{2,1,0:T(8,128)} %get-tuple-element.4) | non-fusion elementwise | flops 40960 | bytes 245760 | tf_op jit(solution)/shard_map/convert_element_type | solution.py:439
  104.8 0.0 copy-done
  104.8 1.6 %bitcast_add_fusion = f32[1,3,32,384]{3,2,1,0:T(8,128)} fusion(f32[3,32,384]{2,1,0:T(8,128)} %get-tuple-element.5, f32[1,3,32,384]{3,2,1,0:T(8,128)S(1)} %copy-done), kind=kLoop, calls=%fused_computation | loop fusion | flops 110592 | bytes 442368 | tf_op jit(solution)/shard_map/add | solution.py:440
Async XLA Ops:
  0.6 104.2 %copy-start = (f32[1,3,32,384]{3,2,1,0:T(8,128)S(1)}, f32[1,3,32,384]{3,2,1,0:T(8,128)}, u32[]{:S(2)}) copy-start(f32[1,3,32,384]{3,2,1,0:T(8,128)} %param.11) | copy-start | bytes 442372

commit v2 on v1

v2 whole, which is shorter than its diff:
```python
import functools
import math

import jax
import jax.numpy as jnp
from jax import lax
from jax.experimental import pallas as pl
from jax.experimental.pallas import tpu as pltpu
from jax.sharding import PartitionSpec as P

MESH = pl.DeviceIdType.MESH
tiny_eps = 1e-06
moment_decay = 0.9
ROWS_FIRST = (((0,), (0,)), ((), ()))
COLS_LAST = (((1,), (1,)), ((), ()))
f32 = jnp.float32
bf16 = jnp.bfloat16


def tile_iotas():
    sub = lax.broadcasted_iota(jnp.int32, (8, 128), 0)
    lane = lax.broadcasted_iota(jnp.int32, (8, 128), 1)
    return sub, lane


def gram_pairs(read, pairs, n, rows, cols, rows_buf):
    used = sorted({k for pair in pairs for k in pair})

    def body(i, accs):
        row = pl.multiple_of(i * 8, 8)
        accs = list(accs)
        for c in range(cols // 128):
            vals = {k: read(k, row, c * 128) for k in used}
            for at, (k, l) in enumerate(pairs):
                accs[at] = accs[at] + vals[k] * vals[l]
        return tuple(accs)

    zero = jnp.zeros((8, 128), f32)
    accs = lax.fori_loop(0, rows // 8, body, tuple(zero for _ in pairs))
    for (k, l), acc in zip(pairs, accs):
        total = jnp.sum(acc, axis=0, keepdims=True)
        for a in range(8):
            for b in range(8):
                if {a % n, b % n} == {k, l}:
                    rows_buf[a * 8 + b : a * 8 + b + 1, :] = total


def gram_tile(rows_buf):
    sub, lane = tile_iotas()
    tile = jnp.zeros((8, 128), f32)
    for b in range(8):
        col = jnp.sum(rows_buf[b * 8 : b * 8 + 8, :], axis=1, keepdims=True)
        tile = tile + jnp.where((lane & 7) == b, col, 0.0)
    return tile


def tree_weights(tile, n):
    sub, lane = tile_iotas()
    weights = jnp.ones((8, 128), f32)
    half = n // 2
    while half >= 1:
        other = (sub + half) & 7
        here_c = jnp.where(lane == sub, tile, 0.0)
        there_c = jnp.where(lane == other, tile, 0.0)
        here_r = jnp.where((lane & 7) == sub, tile, 0.0)
        there_r = jnp.where((lane & 7) == other, tile, 0.0)
        q_col = jnp.maximum(jnp.sum(here_c, axis=1, keepdims=True), 0.0)
        p_col = jnp.sum(there_c, axis=1, keepdims=True)
        q_row = jnp.maximum(jnp.sum(here_r, axis=0, keepdims=True), 0.0)
        p_row = jnp.sum(there_r, axis=0, keepdims=True)
        q_col_b = jnp.broadcast_to(q_col, (8, 128))
        q_row_b = jnp.broadcast_to(q_row, (8, 128))
        most_c = jnp.sqrt(q_col_b) * jnp.sqrt(pltpu.roll(q_col_b, half, 0))
        most_r = jnp.sqrt(q_row_b) * jnp.sqrt(pltpu.roll(q_row_b, half, 1))
        p_col_b = jnp.clip(jnp.broadcast_to(p_col, (8, 128)), -most_c, most_c)
        p_row_b = jnp.clip(jnp.broadcast_to(p_row, (8, 128)), -most_r, most_r)
        coef_c = 1.0 - p_col_b / (2.0 * (q_col_b + tiny_eps))
        coef_r = 1.0 - p_row_b / (2.0 * (q_row_b + tiny_eps))
        weights = weights * coef_c
        tile = tile * coef_c * coef_r
        tile = tile + pltpu.roll(tile, half, 0)
        tile = tile + pltpu.roll(tile, half, 1)
        half //= 2
    return weights


def summed_tiles(buf, at, n, shifted):
    total = buf[0, at]
    for j in range(1, n):
        tile = buf[j, at]
        if shifted:
            tile = pltpu.roll(pltpu.roll(tile, j, 0), j, 1)
        total = total + tile
    return total


def finish(token_ref, comb_ref, mom_ref, token_out, mom_out):
    token_out[...] = token_ref[...].astype(bf16)
    mom_out[0] = moment_decay * mom_ref[0] + (1.0 - moment_decay) * comb_ref[...]


def kernel(
    nx, ny, ne,
    x_ref, cot_ref, gate_ref, route_ref, w_ref,
    token_ref, comb_ref,
    cot_v, gate_v, route_v, w_v, xs, ss, xr, sr, a_buf, g_buf, zs, zr,
    c3_a, c3_b, yr_a, yr_b, yf, st1_a, st1_b, st2_a, st2_b, st3_a, st3_b, rows_buf, wt_buf,
    load_sem, x_sem, xsend, xrecv, asend, arecv, zsend, zrecv,
    ysend, yrecv, s1send, s1recv, s2send, s2recv, s3send, s3recv, near_sem,
):
    rep = lax.axis_index("rep")
    me_e = lax.axis_index("exp")
    me_x = lax.div(rep, ny)
    me_y = lax.rem(rep, ny)
    rows, width = cot_v.shape
    ff = w_v.shape[2]
    dx = width // nx
    dy = dx // ny
    half_w = width // 2
    far = nx // 2

    def x_peer(k):
        return (lax.rem(me_x + k, nx) * ny + me_y, me_e)

    def y_peer(k):
        return (me_x * ny + lax.rem(me_y + k, ny), me_e)

    def e_peer(k):
        return (rep, lax.rem(me_e + k, ne))

    chips = ne // 2
    chip = lax.div(me_e, 2)
    place = jnp.where(lax.rem(me_e, 2) == 0, chip, ne - 1 - chip)

    def on_line(at):
        return (rep, jnp.where(at < chips, 2 * at, 2 * (ne - 1 - at) + 1))

    def line_signal(sem, reach):
        @pl.when(place >= reach)
        def _():
            pl.semaphore_signal(sem, inc=1, device_id=on_line(place - reach), device_id_type=MESH)

        @pl.when(place + reach < ne)
        def _():
            pl.semaphore_signal(sem, inc=1, device_id=on_line(place + reach), device_id_type=MESH)

    def line_count(reach):
        return (place >= reach).astype(jnp.int32) + (place + reach < ne).astype(jnp.int32)

    cot_load = pltpu.make_async_copy(cot_ref.at[0], cot_v, load_sem.at[0])
    cot_load.start()
    gate_load = pltpu.make_async_copy(gate_ref, gate_v, load_sem.at[4])
    gate_load.start()
    x_loads = []
    for j in range(nx):
        load = pltpu.make_async_copy(x_ref.at[0, :, pl.ds(j * dx, dx)], xs.at[j], x_sem.at[j])
        load.start()
        x_loads.append(load)
    w_loads = []
    for t in range(3):
        load = pltpu.make_async_copy(w_ref.at[0, t], w_v.at[t], load_sem.at[1 + t])
        load.start()
        w_loads.append(load)
    route_load = pltpu.make_async_copy(route_ref, route_v, load_sem.at[5])
    route_load.start()

    barrier = pltpu.get_barrier_semaphore()
    peers = [x_peer(k) for k in range(1, nx)]
    peers += [y_peer(k) for k in range(1, ny)]
    for peer in peers:
        pl.semaphore_signal(barrier, inc=1, device_id=peer, device_id_type=MESH)

    line_signal(barrier, 1)

    eye = lax.broadcasted_iota(jnp.int32, (rows, rows), 0) == lax.broadcasted_iota(
        jnp.int32, (rows, rows), 1
    )
    cot_load.wait()
    gate_load.wait()
    gate_col = jnp.sum(jnp.where(eye, gate_v[...], 0.0), axis=1, keepdims=True)
    for j in range(nx):
        ss[j] = (gate_col * cot_v[:, j * dx : (j + 1) * dx].astype(f32)).astype(bf16)

    for load in x_loads:
        load.wait()
    w_loads[0].wait()
    w_loads[1].wait()
    gate_pre = jnp.zeros((rows, ff), f32)
    up_pre = jnp.zeros((rows, ff), f32)
    for j in range(nx):
        part = xs[j]
        gate_pre += jnp.dot(part, w_v[0, j * dx : (j + 1) * dx, :], preferred_element_type=f32)
        up_pre += jnp.dot(part, w_v[1, j * dx : (j + 1) * dx, :], preferred_element_type=f32)
    sigma = 1.0 / (1.0 + jnp.exp(-gate_pre))
    act = gate_pre * sigma
    a_buf[0, 0] = (act * up_pre).astype(bf16)
    w_loads[2].wait()
    hidden_grad = jnp.zeros((rows, ff), f32)
    for j in range(nx):
        hidden_grad += jnp.dot(ss[j], w_v[2, j * dx : (j + 1) * dx, :], preferred_element_type=f32)
    a_buf[1, 0] = (hidden_grad * up_pre * sigma * (1.0 + gate_pre * (1.0 - sigma))).astype(bf16)
    a_buf[2, 0] = (hidden_grad * act).astype(bf16)
    sr[0] = ss[me_x]
    xr[0] = xs[me_x]

    pl.semaphore_wait(barrier, len(peers) + line_count(1))

    def send(src, dst, ssem, rsem, peer):
        copy = pltpu.make_async_remote_copy(
            src_ref=src, dst_ref=dst, send_sem=ssem, recv_sem=rsem,
            device_id=peer, device_id_type=MESH,
        )
        copy.start()

    def wait_bytes(ref, sem):
        pltpu.make_async_copy(ref, ref, sem).wait()

    order_x = sorted(range(1, nx), key=lambda k: -min(k, nx - k))
    order_y = sorted(range(1, ny), key=lambda k: -min(k, ny - k))

    def ring_parts(step):
        parts = []
        if step < far:
            parts.append(((nx - step + 1) % nx, nx - step, 0, rows, 1))
            parts.append((step - 1, step, 0, rows, nx - 1))
        else:
            parts.append(((nx - step + 1) % nx, far, 0, rows // 2, 1))
            parts.append((step - 1, far, rows // 2, rows // 2, nx - 1))
        return parts

    def ring_refs(t, step):
        found = []
        for way, (src, dst, first, count, offset) in enumerate(ring_parts(step)):
            found.append((
                a_buf.at[t, src, pl.ds(first, count)],
                a_buf.at[t, dst, pl.ds(first, count)],
                (t * far + step - 1) * 2 + way,
                offset,
            ))
        return found

    def ring_wait(t, step):
        for src, dst, at, offset in ring_refs(t, step):
            wait_bytes(dst, arecv.at[at])

    def ring_step(t, step):
        if step > 1:
            ring_wait(t, step - 1)
        for src, dst, at, offset in ring_refs(t, step):
            send(src, dst, asend.at[at], arecv.at[at], x_peer(offset))

    nearest = []
    for k in range(1, far):
        nearest += [k, nx - k]
    nearest.append(far)
    cuts = (0, (len(nearest) + 1) * 3 // 8, (len(nearest) + 1) * 5 // 8, len(nearest))

    def send_left(t, piece):
        mine, there = (ss, sr) if t == 0 else (xs, xr)
        for k in nearest[cuts[piece] : cuts[piece + 1]]:
            send(mine.at[lax.rem(me_x + k, nx)], there.at[nx - k], xsend.at[t], xrecv.at[t, nx - k], x_peer(k))

    def wait_left(t, slots):
        for k in slots:
            wait_bytes((sr, xr)[t].at[k], xrecv.at[t, k])

    def near(index):
        if 0 < index <= len(reaches):
            pl.semaphore_wait(near_sem.at[index - 1], line_count(reaches[index - 1]))
        if index < len(reaches):
            line_signal(near_sem.at[index], reaches[index])

    reaches = [1 << i for i in range(8) if 1 << i < ne - 1]

    def row_grads():
        gate_grad = a_buf[1, 0]
        up_grad = a_buf[2, 0]
        blk = min(256, half_w)

        def piece(col):
            at = pl.ds(pl.multiple_of(col, blk), blk)
            val = lax.dot_general(gate_grad, w_v[0, at, :], COLS_LAST, preferred_element_type=f32)
            val += lax.dot_general(up_grad, w_v[1, at, :], COLS_LAST, preferred_element_type=f32)
            return val.reshape(ne, rows // ne, blk)

        def body(j, carry):
            both = jnp.concatenate([piece(j * blk), piece(half_w + j * blk)], axis=1)
            zs[:, :, pl.ds(pl.multiple_of(j * blk, blk), blk)] = both.astype(bf16)
            return carry

        lax.fori_loop(0, half_w // blk, body, 0)

    def send_rows():
        for k in range(1, ne):
            send(zs.at[lax.rem(me_e + k, ne)], zr.at[ne - k], zsend.at[0], zrecv.at[0], e_peer(k))
        zr[0] = zs[me_e]

    def tokens():
        wait_bytes(zr.at[pl.ds(1, ne - 1)], zrecv.at[0])
        route_load.wait()
        cap = rows // ne
        tall = ne * 2 * cap
        count = token_ref.shape[1]
        route = route_v[0]
        at = ((lax.div(route, cap) - me_e + ne) & (ne - 1)) * (2 * cap) + lax.rem(route, cap)
        col = lax.broadcasted_iota(jnp.int32, (count, tall), 1)
        low = jnp.zeros((count, tall), f32)
        high = jnp.zeros((count, tall), f32)
        for k in range(route.shape[1]):
            low += jnp.where(col == at[:, k : k + 1], 1.0, 0.0)
            high += jnp.where(col == at[:, k : k + 1] + cap, 1.0, 0.0)
        got = zr[...].reshape(tall, half_w)
        token_ref[0, :, :half_w] = jnp.dot(low.astype(bf16), got, preferred_element_type=f32)
        token_ref[0, :, half_w:] = jnp.dot(high.astype(bf16), got, preferred_element_type=f32)

    groups = ((0,), (1, 2))
    st1, st2, st3 = (st1_a, st1_b), (st2_a, st2_b), (st3_a, st3_b)
    c3, yr = (c3_a, c3_b), (yr_a, yr_b)
    known = {t: [] for t in range(3)}

    def product(t, steps):
        left = sr if t == 0 else xr
        fresh = []
        for step in steps:
            fresh += [step] if step in (0, far) else [step, nx - step]
        for k in fresh:
            g_buf[t, k] = lax.dot_general(left[k], a_buf[t, k], ROWS_FIRST, preferred_element_type=f32)

        def read(k, row, col):
            return g_buf[t, k, pl.ds(row, 8), col : col + 128]

        both = known[t] + fresh
        pairs = [(k, l) for at, k in enumerate(both) for l in both[at:] if l in fresh]
        gram_pairs(read, pairs, nx, dx, ff, rows_buf.at[t])
        known[t] = both

    def combine_1(g):
        for at, t in enumerate(groups[g]):
            st1[g][0, at] = gram_tile(rows_buf.at[t])
        for k in order_x:
            send(st1[g].at[0], st1[g].at[nx - k], s1send.at[g], s1recv.at[g], x_peer(k))

    def combine_2(g):
        wait_bytes(st1[g].at[pl.ds(1, nx - 1)], s1recv.at[g])
        parts = dy // 16
        for at, t in enumerate(groups[g]):
            wt_buf[at] = tree_weights(summed_tiles(st1[g], at, nx, True), nx)
            lanes = [wt_buf[at, k : k + 1, :] for k in range(nx)]

            def body(i, carry, at=at, t=t, lanes=lanes):
                src = pl.ds(pl.multiple_of(i * 16, 16), 16)
                dst = pl.ds(pl.multiple_of(lax.rem(i, parts) * 16, 16), 16)
                for c in range(ff // 128):
                    cols = slice(c * 128, c * 128 + 128)
                    total = lanes[0] * g_buf[t, 0, src, cols]
                    for k in range(1, nx):
                        total = total + lanes[k] * g_buf[t, k, src, cols]
                    c3[g][lax.div(i, parts), at, dst, cols] = total.astype(bf16)
                return carry

            lax.fori_loop(0, dx // 16, body, 0)
        for k in order_y:
            send(c3[g].at[lax.rem(me_y + k, ny)], yr[g].at[ny - k], ysend.at[g], yrecv.at[g], y_peer(k))
        yr[g][0] = c3[g][me_y]

    def combine_3(g):
        wait_bytes(yr[g].at[pl.ds(1, ny - 1)], yrecv.at[g])
        pairs = [(k, l) for k in range(ny) for l in range(k, ny)]
        for at, t in enumerate(groups[g]):
            for k in range(ny):
                yf[t, k] = yr[g][k, at].astype(f32)

            def read(k, row, col, t=t):
                return yf[t, k, pl.ds(row, 8), col : col + 128]

            gram_pairs(read, pairs, ny, dy, ff, rows_buf.at[t])
            st2[g][0, at] = gram_tile(rows_buf.at[t])
        for k in order_x:
            send(st2[g].at[0], st2[g].at[nx - k], s2send.at[g], s2recv.at[g], x_peer(k))

    def combine_4(g):
        wait_bytes(st2[g].at[pl.ds(1, nx - 1)], s2recv.at[g])
        for at, t in enumerate(groups[g]):
            st3[g][0, at] = summed_tiles(st2[g], at, nx, False)
        for k in order_y:
            send(st3[g].at[0], st3[g].at[ny - k], s3send.at[g], s3recv.at[g], y_peer(k))

    def combine_5(g):
        wait_bytes(st3[g].at[pl.ds(1, ny - 1)], s3recv.at[g])
        for at, t in enumerate(groups[g]):
            wt_buf[at] = tree_weights(summed_tiles(st3[g], at, ny, True), ny)
            for c in range(ff // 128):
                cols = slice(c * 128, c * 128 + 128)
                total = wt_buf[at, 0:1, :] * yf[t, 0, :, cols]
                for k in range(1, ny):
                    total = total + wt_buf[at, k : k + 1, :] * yf[t, k, :, cols]
                comb_ref[(t + 2) % 3, :, cols] = total

    def steps(tensors, step):
        if step <= far:
            for t in tensors:
                ring_step(t, step)

    near(0)
    steps((1, 2), 1)
    send_left(1, 0)
    row_grads()
    steps((1, 2), 2)
    send_left(1, 1)
    near(1)
    steps((1, 2), 3)
    send_left(1, 2)
    steps((0,), 1)
    near(2)
    steps((1, 2), 4)
    send_left(0, 0)
    wait_left(1, nearest)
    product(1, range(far))
    steps((0,), 2)
    send_left(0, 1)
    product(2, range(far))
    near(3)
    ring_wait(1, far)
    ring_wait(2, far)
    steps((0,), 3)
    send_left(0, 2)
    product(1, [far])
    product(2, [far])
    combine_1(1)
    steps((0,), 4)
    near(4)
    send_rows()
    combine_2(1)
    wait_left(0, nearest[:-1])
    product(0, range(far))
    combine_3(1)
    wait_left(0, nearest[-1:])
    ring_wait(0, far)
    product(0, [far])
    combine_1(0)
    combine_4(1)
    combine_2(0)
    combine_5(1)
    combine_3(0)
    combine_4(0)
    tokens()
    combine_5(0)

    for t, ref in enumerate((sr, xr)):
        wait_bytes(ref.at[pl.ds(1, nx - 1)], xsend.at[t])
    for t in range(3):
        for step in range(1, far + 1):
            for src, dst, at, offset in ring_refs(t, step):
                wait_bytes(src, asend.at[at])
    for g in range(2):
        wait_bytes(st1[g].at[pl.ds(1, nx - 1)], s1send.at[g])
        wait_bytes(yr[g].at[pl.ds(1, ny - 1)], ysend.at[g])
        wait_bytes(st2[g].at[pl.ds(1, nx - 1)], s2send.at[g])
        wait_bytes(st3[g].at[pl.ds(1, ny - 1)], s3send.at[g])
    wait_bytes(zr.at[pl.ds(1, ne - 1)], zsend.at[0])


def on_device(nx, ny, ne, x_rows, row_cot, gate_vals, route_pos, weights, momentum):
    rows, width = x_rows.shape[1:]
    ff = weights.shape[3]
    dx = width // nx
    dy = dx // ny
    far = nx // 2
    tokens = route_pos.shape[1]
    vmem = pltpu.VMEM
    dma = pltpu.SemaphoreType.DMA
    in_hbm = pl.BlockSpec(memory_space=pl.ANY)
    in_vmem = pl.BlockSpec(memory_space=pltpu.VMEM)
    token_sum, combined = pl.pallas_call(
        functools.partial(kernel, nx, ny, ne),
        out_shape=(
            jax.ShapeDtypeStruct((1, tokens, width), f32),
            jax.ShapeDtypeStruct((3, dy, ff), f32),
        ),
        in_specs=[in_hbm] * 5,
        out_specs=(in_vmem, in_vmem),
        scratch_shapes=[
            vmem((rows, width), bf16),
            vmem(gate_vals.shape, f32),
            vmem(route_pos.shape, jnp.int32),
            vmem((3, width, ff), bf16),
            vmem((nx, rows, dx), bf16),
            vmem((nx, rows, dx), bf16),
            vmem((nx, rows, dx), bf16),
            vmem((nx, rows, dx), bf16),
            vmem((3, nx, rows, ff), bf16),
            vmem((3, nx, dx, ff), f32),
            vmem((ne, 2 * rows // ne, width // 2), bf16),
            vmem((ne, 2 * rows // ne, width // 2), bf16),
            vmem((ny, 1, dy, ff), bf16),
            vmem((ny, 2, dy, ff), bf16),
            vmem((ny, 1, dy, ff), bf16),
            vmem((ny, 2, dy, ff), bf16),
            vmem((3, ny, dy, ff), f32),
            vmem((nx, 1, 8, 128), f32),
            vmem((nx, 2, 8, 128), f32),
            vmem((nx, 1, 8, 128), f32),
            vmem((nx, 2, 8, 128), f32),
            vmem((ny, 1, 8, 128), f32),
            vmem((ny, 2, 8, 128), f32),
            vmem((3, 64, 128), f32),
            vmem((2, 8, 128), f32),
            dma((6,)),
            dma((nx,)),
            dma((2,)),
            dma((2, nx)),
            dma((6 * far,)),
            dma((6 * far,)),
            dma((1,)),
            dma((1,)),
            dma((2,)),
            dma((2,)),
            dma((2,)),
            dma((2,)),
            dma((2,)),
            dma((2,)),
            dma((2,)),
            dma((2,)),
            pltpu.SemaphoreType.REGULAR((8,)),
        ],
        compiler_params=pltpu.CompilerParams(
            collective_id=0, has_side_effects=True, vmem_limit_bytes=56 * 1024 * 1024
        ),
        cost_estimate=pl.CostEstimate(
            flops=16 * rows * width * ff, bytes_accessed=2 * (3 * width * ff + 2 * rows * width),
            transcendentals=rows * ff,
        ),
    )(x_rows, row_cot, gate_vals, route_pos, weights)
    token_grad, momentum_new = pl.pallas_call(
        finish,
        out_shape=(
            jax.ShapeDtypeStruct(token_sum.shape, bf16),
            jax.ShapeDtypeStruct(momentum.shape, f32),
        ),
        in_specs=[in_vmem] * 3,
        out_specs=(in_vmem, in_vmem),
    )(token_sum, combined, momentum)
    return (token_grad, momentum_new)


def solution(mesh):
    reps, ne = mesh.shape["rep"], mesh.shape["exp"]
    nx = 1 << ((reps.bit_length()) // 2)
    ny = reps // nx
    placed = (
        P("rep", "exp", None),
        P("rep", "exp", None),
        P("rep", "exp"),
        P("rep", "exp", None),
        P("exp", None, None, None),
        P("exp", None, "rep", None),
    )
    return jax.shard_map(
        functools.partial(on_device, nx, ny, ne),
        mesh=mesh,
        in_specs=placed,
        out_specs=(P("rep", "exp", None), P("exp", None, "rep", None)),
        check_vma=False,
    )
```

time: 107 us -> 98.3 us (0.919)
  Pallas kernels: 101 us -> 96.1 us
  other arithmetic: 3.17 us -> 0 us
    pallas_call x1, Pallas kernels: 101 us -> 94.4 us  [on_device(): pl.pallas_call(functools.partial(kernel, nx, ny, ne), out_shape=(jax.Shap...]
    pallas_call x0 -> x1, Pallas kernels: none -> 1.78 us  [on_device(): pl.pallas_call(finish, out_shape=(jax.ShapeDtypeStruct(token_sum.shape, b...]
    add x1 -> x0, other arithmetic: 1.6 us -> none  [on_device(): moment_decay * momentum + (1.0 - moment_decay) * combined[None]]
    convert_element_type x1 -> x0, other arithmetic: 1.58 us -> none  [on_device(): token_grad = token_sum.astype(bf16)]
where the time goes in v2:
time: 98.3 us; the launch traced here: 98.2 us
  Pallas kernels  96.1 us (98%)
  local copies, waits for them, and re-layouts  1.36 us (1%)
    pallas_call x1, Pallas kernels, on_device(): pl.pallas_call(functools.partial(kernel, nx, ny, ne), out_shape=(jax.Shap...  94.4 us

profile of v2, /device:TPU:2, one launch (start us, length us, event | category | flops | bytes accessed | tf_op | source)
XLA Modules:
  0.0 98.2 jit_solution(9622762473110849910)
XLA Ops:
  0.6 1.4 %copy.8.route_ref = s32[1,20,4]{2,1,0:T(8,128)} copy(s32[1,20,4]{1,2,0:T(4,128)} %param.9) | data formatting | bytes 640 | tf_op args[3]
  2.0 94.4 %shard_map.77 = (f32[1,20,2048]{2,1,0:T(8,128)}, f32[3,32,384]{2,1,0:T(8,128)}) custom-call(bf16[1,128,2048]{2,1,0:T(8,128)(2,1)} %x_ref.1, bf16[1,128,2048]{2,1,0:T(8,128)(2,1)} %cot_ref.1, f32[1,128]{1,0:T(1,128)} %gate_ref.1, s32[1,20,4]{2,1,0:T(8,128)} %copy.8.route_ref, bf16[1,3,2048,384]{3,2,1,0:T(8,128)(2,1)} %w_ref.1), custom_call_target="tpu_custom_call" | custom-call | flops 1610612736 | bytes 5767168 | tf_op jit(solution)/shard_map/pallas_call | solution.py:474
  96.4 1.8 %shard_map.78 = (bf16[1,20,2048]{2,1,0:T(8,128)(2,1)}, f32[1,3,32,384]{3,2,1,0:T(8,128)}) custom-call(f32[1,20,2048]{2,1,0:T(8,128)} %get-tuple-element.4.token_ref, f32[3,32,384]{2,1,0:T(8,128)} %get-tuple-element.5.comb_ref, f32[1,3,32,384]{3,2,1,0:T(8,128)} %mom_ref.1), custom_call_target="tpu_custom_call" | custom-call | tf_op jit(solution)/shard_map/pallas_call | solution.py:534

commit v3 on v2

--- a/solution.py
+++ b/solution.py
@@ -303,15 +303,17 @@
         count = token_ref.shape[1]
         route = route_v[0]
         at = ((lax.div(route, cap) - me_e + ne) & (ne - 1)) * (2 * cap) + lax.rem(route, cap)
-        col = lax.broadcasted_iota(jnp.int32, (count, tall), 1)
-        low = jnp.zeros((count, tall), f32)
-        high = jnp.zeros((count, tall), f32)
-        for k in range(route.shape[1]):
-            low += jnp.where(col == at[:, k : k + 1], 1.0, 0.0)
-            high += jnp.where(col == at[:, k : k + 1] + cap, 1.0, 0.0)
+        row = lax.broadcasted_iota(jnp.int32, (tall, count), 0)
+        low = jnp.zeros((tall, count), f32)
+        high = jnp.zeros((tall, count), f32)
+        for k in range(route.shape[0]):
+            low += jnp.where(row == at[k : k + 1, :], 1.0, 0.0)
+            high += jnp.where(row == at[k : k + 1, :] + cap, 1.0, 0.0)
         got = zr[...].reshape(tall, half_w)
-        token_ref[0, :, :half_w] = jnp.dot(low.astype(bf16), got, preferred_element_type=f32)
-        token_ref[0, :, half_w:] = jnp.dot(high.astype(bf16), got, preferred_element_type=f32)
+        for picks, cols in ((low, slice(0, half_w)), (high, slice(half_w, width))):
+            token_ref[0, :, cols] = lax.dot_general(
+                picks.astype(bf16), got, ROWS_FIRST, preferred_element_type=f32
+            )
 
     groups = ((0,), (1, 2))
     st1, st2, st3 = (st1_a, st1_b), (st2_a, st2_b), (st3_a, st3_b)
@@ -402,50 +404,45 @@
                 ring_step(t, step)
 
     near(0)
-    steps((1, 2), 1)
-    send_left(1, 0)
+    steps((1, 2, 0), 1)
+    for piece in range(3):
+        send_left(1, piece)
+    send_left(0, 0)
     row_grads()
-    steps((1, 2), 2)
-    send_left(1, 1)
     near(1)
-    steps((1, 2), 3)
-    send_left(1, 2)
-    steps((0,), 1)
+    steps((1, 2, 0), 2)
+    send_left(0, 1)
+    send_left(0, 2)
     near(2)
-    steps((1, 2), 4)
-    send_left(0, 0)
+    steps((1, 2, 0), 3)
     wait_left(1, nearest)
-    product(1, range(far))
-    steps((0,), 2)
-    send_left(0, 1)
-    product(2, range(far))
+    product(1, range(far - 1))
+    product(2, range(far - 1))
+    wait_left(0, nearest)
+    product(0, range(far - 1))
     near(3)
+    steps((1, 2, 0), 4)
+    product(1, [far - 1])
+    product(2, [far - 1])
+    product(0, [far - 1])
     ring_wait(1, far)
     ring_wait(2, far)
-    steps((0,), 3)
-    send_left(0, 2)
     product(1, [far])
     product(2, [far])
     combine_1(1)
-    steps((0,), 4)
+    ring_wait(0, far)
+    product(0, [far])
+    combine_1(0)
     near(4)
     send_rows()
     combine_2(1)
-    wait_left(0, nearest[:-1])
-    product(0, range(far))
+    combine_2(0)
     combine_3(1)
-    wait_left(0, nearest[-1:])
-    ring_wait(0, far)
-    product(0, [far])
-    combine_1(0)
+    combine_3(0)
     combine_4(1)
-    combine_2(0)
+    combine_4(0)
     combine_5(1)
-    combine_3(0)
-    combine_4(0)
     tokens()
-    combine_5(0)
-
     for t, ref in enumerate((sr, xr)):
         wait_bytes(ref.at[pl.ds(1, nx - 1)], xsend.at[t])
     for t in range(3):
@@ -458,6 +455,7 @@
         wait_bytes(st2[g].at[pl.ds(1, nx - 1)], s2send.at[g])
         wait_bytes(st3[g].at[pl.ds(1, ny - 1)], s3send.at[g])
     wait_bytes(zr.at[pl.ds(1, ne - 1)], zsend.at[0])
+    combine_5(0)
 
 
 def on_device(nx, ny, ne, x_rows, row_cot, gate_vals, route_pos, weights, momentum):
@@ -467,6 +465,7 @@
     dy = dx // ny
     far = nx // 2
     tokens = route_pos.shape[1]
+    by_choice = jnp.swapaxes(route_pos, 1, 2)
     vmem = pltpu.VMEM
     dma = pltpu.SemaphoreType.DMA
     in_hbm = pl.BlockSpec(memory_space=pl.ANY)
@@ -482,7 +481,7 @@
         scratch_shapes=[
             vmem((rows, width), bf16),
             vmem(gate_vals.shape, f32),
-            vmem(route_pos.shape, jnp.int32),
+            vmem(by_choice.shape, jnp.int32),
             vmem((3, width, ff), bf16),
             vmem((nx, rows, dx), bf16),
             vmem((nx, rows, dx), bf16),
@@ -530,7 +529,7 @@
             flops=16 * rows * width * ff, bytes_accessed=2 * (3 * width * ff + 2 * rows * width),
             transcendentals=rows * ff,
         ),
-    )(x_rows, row_cot, gate_vals, route_pos, weights)
+    )(x_rows, row_cot, gate_vals, by_choice, weights)
     token_grad, momentum_new = pl.pallas_call(
         finish,
         out_shape=(

time: 98.3 us -> 93.1 us (0.947)
  Pallas kernels: 96.1 us -> 92.3 us
  local copies, waits for them, and re-layouts: 1.36 us -> 0 us
    pallas_call x1, Pallas kernels: 94.4 us -> 90.5 us  [on_device(): pl.pallas_call(functools.partial(kernel, nx, ny, ne), out_shape=(jax.Shap...]
    unnamed x1 -> x0, local copies, waits for them, and re-layouts: 1.36 us -> none
where the time goes in v3:
time: 93.1 us; the launch traced here: 93 us
  Pallas kernels  92.3 us (99%)
    pallas_call x1, Pallas kernels, on_device(): pl.pallas_call(functools.partial(kernel, nx, ny, ne), out_shape=(jax.Shap...  90.5 us

profile of v3, /device:TPU:2, one launch (start us, length us, event | category | flops | bytes accessed | tf_op | source)
XLA Modules:
  0.0 93.0 jit_solution(11584547358397633899)
XLA Ops:
  0.6 90.5 %shard_map.77 = (f32[1,20,2048]{2,1,0:T(8,128)}, f32[3,32,384]{2,1,0:T(8,128)}) custom-call(bf16[1,128,2048]{2,1,0:T(8,128)(2,1)} %x_ref.1, bf16[1,128,2048]{2,1,0:T(8,128)(2,1)} %cot_ref.1, f32[1,128]{1,0:T(1,128)} %gate_ref.1, s32[1,4,20]{2,1,0:T(4,128)} %bitcast.1, bf16[1,3,2048,384]{3,2,1,0:T(8,128)(2,1)} %w_ref.1), custom_call_target="tpu_custom_call" | custom-call | flops 1610612736 | bytes 5767168 | tf_op jit(solution)/shard_map/pallas_call | solution.py:473
  91.2 1.8 %shard_map.78 = (bf16[1,20,2048]{2,1,0:T(8,128)(2,1)}, f32[1,3,32,384]{3,2,1,0:T(8,128)}) custom-call(f32[1,20,2048]{2,1,0:T(8,128)} %get-tuple-element.4.token_ref, f32[3,32,384]{2,1,0:T(8,128)} %get-tuple-element.5.comb_ref, f32[1,3,32,384]{3,2,1,0:T(8,128)} %mom_ref.1), custom_call_target="tpu_custom_call" | custom-call | tf_op jit(solution)/shard_map/pallas_call | solution.py:533
